TPU v7x, 32 devices: a whole 2x2x4 slice. The times are simulated.
32 devices in a mesh: lon: 8 (over z, y), lat: 4 (over x, core).
Axes of the slice: x: 2, y: 2, z: 4, core: 2. Of those that a mesh axis runs over, the one named last changes fastest.
Arguments:
- adjoint_final: float32 [10, 256, 2048], P(None, 'lat', 'lon'), may hold values from -6 to 6
- stored_tracer: float32 [4, 10, 256, 2048], P(None, None, 'lat', 'lon'), may hold values from -4 to 4
- stored_zonal: float32 [4, 10, 256, 2048], P(None, None, 'lat', 'lon'), may hold values from -4 to 4
- stored_meridional: float32 [4, 10, 256, 2048], P(None, None, 'lat', 'lon'), may hold values from -4 to 4
- diffusivity: float32 [256, 2048], P('lat', 'lon'), may hold values from 0.02 to 0.2
- level_mixing: float32 [10, 10], replicated, may hold values from -2 to 2
- wet_tiles: int32 [4, 16], P('lat', 'lon'), may hold values 0 or 1
- state_index: int32 [2], replicated, may hold values from 0 to 3, as said below
Outputs:
- adjoint_start: float32 [10, 256, 2048], P(None, 'lat', 'lon')
Inputs may be any that keep to these rules, and one draw needn't show every extreme that they name: The entries of state_index are distinct stored states, and one of them is the last stored state.
All inputs are finite; a program needn't handle non-finite values. No bound on the sum of `wet_tiles` on one device may be relied on, other than what follows from the above.
Results may differ from a plain program's by a relative error of at most 0.0001.
Values sent between devices are 32-bit elements; how exact they have to be, the bound alone decides.
A program may use at most 64 MiB of HBM per device.

v0:
```python
import jax
import jax.numpy as jnp
from jax import lax
from jax.sharding import PartitionSpec as P

TLON = 128
STEPS = 2


advect_scale = 0.25
damping = 0.3


def partner(array, axis, distance):
    return lax.ppermute(array, axis, [(i, i ^ 1 << distance) for i in range(lax.axis_size(axis))])


def with_halo(block, sides, width, periodic):
    for axis, dim in sides:
        count = lax.axis_size(axis)
        forward = [(i, i + 1) for i in range(count - 1)]
        if periodic:
            forward.append((count - 1, 0))
        backward = [(target, source) for source, target in forward]
        low = lax.ppermute(
            lax.slice_in_dim(block, block.shape[dim] - width, None, axis=dim), axis, forward
        )
        high = lax.ppermute(lax.slice_in_dim(block, 0, width, axis=dim), axis, backward)
        block = jnp.concatenate([low, block, high], axis=dim)
    return block


def folded_rows(top_rows):
    bit_count = lax.axis_size("lon").bit_length() - 1
    moved = top_rows
    for bit_index in range(bit_count):
        moved = partner(moved, "lon", bit_index)
    return moved[..., ::-1]


def shards(
    adjoint_final,
    stored_tracer,
    stored_zonal,
    stored_meridional,
    diffusivity,
    level_mixing,
    wet_tiles,
    state_index,
):
    wet = jnp.repeat(wet_tiles[0], TLON).astype(jnp.float32)[None, None, :]
    is_top = lax.axis_index("lat") == lax.axis_size("lat") - 1
    adjoint = adjoint_final * wet
    for back in range(STEPS):
        chosen = state_index[STEPS - 1 - back]
        tracer = stored_tracer[chosen]
        zonal = stored_zonal[chosen]
        merid = stored_meridional[chosen]
        spread = diffusivity[None] * adjoint
        zonal_flux = zonal * adjoint
        merid_flux = merid * adjoint
        along_lon = with_halo(jnp.stack([spread, zonal_flux]), (("lon", 3),), 1, True)
        along_lat_src = jnp.stack([spread, merid_flux])
        along_lat = with_halo(along_lat_src, (("lat", 2),), 1, False)
        mirrored = folded_rows(along_lat_src[:, :, -1, :])
        last_north = jnp.where(is_top, mirrored, along_lat[:, :, -1, :])
        north_side = jnp.concatenate([along_lat[:, :, 2:-1, :], last_north[:, :, None, :]], axis=2)
        south_side = along_lat[:, :, :-2, :]
        east_side = along_lon[..., 2:]
        west_side = along_lon[..., :-2]
        nearby = east_side[0] + west_side[0] + north_side[0] + south_side[0]
        advect = east_side[1] - west_side[1] + north_side[1] - south_side[1]
        vertical = jnp.einsum("ml,mab->lab", level_mixing, adjoint, precision=lax.Precision.HIGHEST)
        adjoint = wet * (
            adjoint
            - 4.0 * spread
            + nearby
            + advect_scale * advect
            + vertical
            - damping * tracer * tracer * adjoint
        )
    return adjoint


def solution(mesh):
    return jax.shard_map(
        shards,
        mesh=mesh,
        in_specs=(
            P(None, "lat", "lon"),
            P(None, None, "lat", "lon"),
            P(None, None, "lat", "lon"),
            P(None, None, "lat", "lon"),
            P("lat", "lon"),
            P(),
            P("lat", "lon"),
            P(),
        ),
        out_specs=P(None, "lat", "lon"),
        check_vma=False,
    )
```

profile of v0, /device:TPU:1, one launch (start us, length us, event | category | flops | bytes accessed | tf_op | source)
XLA Modules:
  0.0 71.1 jit_solution(4836353650015378590)
XLA Ops:
  0.0 1.4 %fusion.50 = (s32[1]{0:T(128)}, s32[1]{0:T(128)}) fusion(s32[2]{0:T(128)} %param.15), kind=kLoop, calls=%fused_computation.106 | loop fusion | bytes 16 | tf_op jit(solution)/shard_map/slice | solution.py:55
  4.0 0.7 convert_bitcast_fusion
  4.6 0.1 broadcast_bitcast_fusion
  6.0 0.0 copy-start.9
  6.0 0.0 copy-start.10
  6.0 3.1 %constant_dynamic-slice_fusion.1 = (f32[1,10,64,256]{3,2,1,0:T(8,128)}, f32[1,10,64,256]{3,2,1,0:T(8,128)S(1)}, f32[1,10,64,256]{3,2,1,0:T(8,128)S(1)}, f32[1,10,64,256]{3,2,1,0:T(8,128)}) fusion(f32[4,10,64,256]{3,2,1,0:T(8,128)} %param.11, s32[]{:T(128)S(6)} %select_n.25, s32[]{:T(128)S(6)} %select_n.22, f32[4,10,64,256]{3,2,1,0:T(8,128)} %param.10), kind=kLoop, calls=%fused_computation.99 | loop fusion | bytes 5242888 | tf_op jit(solution)/shard_map/dynamic_slice | solution.py:58
  9.1 0.0 copy-done.10
  9.1 1.2 %fusion.37 = (f32[1,10,64,256]{3,1,2,0:T(8,128)S(1)}, f32[1,10,64,256]{3,1,2,0:T(8,128)S(1)}, f32[1,10,64,256]{3,1,2,0:T(8,128)S(1)}) fusion(f32[1,10,64,256]{3,2,1,0:T(8,128)S(1)} %get-tuple-element.27, f32[10,64,256]{2,1,0:T(8,128)S(1)} %copy-done.9, f32[256]{0:T(256)S(1)} %broadcast_bitcast_fusion, f32[1,10,64,256]{3,2,1,0:T(8,128)S(1)} %get-tuple-element.10, ...), kind=kLoop, calls=%fused_computation.79 | loop fusion | flops 655360 | bytes 3998720 | tf_op jit(solution)/shard_map/stack | solution.py:62
  10.3 4.5 %collective-permute-start.6 = (f32[2,10,1,256]{3,1,0,2:T(8,128)S(1)}, f32[2,10,1,256]{3,1,0,2:T(8,128)S(1)}, u32[]{:S(2)}, u32[]{:S(2)}) collective-permute-start(f32[2,10,1,256]{3,1,0,2:T(8,128)S(1)} %bitcast.111), channel_id=1, source_target_pairs={{0,1},{1,2},{2,3},{4,5},{5,6},{6,7},{8,9},{9,10},{10,11},{12,13},{... | collective-permute-start | bytes 61448 | tf_op jit(solution)/shard_map/ppermute | solution.py:25
  14.8 1.3 %collective-permute-start.2 = (f32[2,10,256]{2,1,0:T(8,128)S(1)}, f32[2,10,256]{2,1,0:T(8,128)S(1)}, u32[]{:S(2)}, u32[]{:S(2)}) collective-permute-start(f32[2,10,256]{2,1,0:T(8,128)S(1)} %bitcast.112), channel_id=1, source_target_pairs={{0,4},{4,0},{8,12},{12,8},{16,20},{20,16},{24,28},{28,24},{1,5},{5... | collective-permute-start | bytes 61448 | tf_op jit(solution)/shard_map/ppermute | solution.py:15
  16.1 1.9 %collective-permute-start.5 = (f32[2,10,1,256]{3,1,0,2:T(8,128)S(1)}, f32[2,10,1,256]{3,1,0,2:T(8,128)S(1)}, u32[]{:S(2)}, u32[]{:S(2)}) collective-permute-start(f32[2,10,1,256]{3,1,0,2:T(8,128)S(1)} %get-tuple-element.17), channel_id=1, source_target_pairs={{1,0},{2,1},{3,2},{5,4},{6,5},{7,6},{9,8},{10,9},{11,10},{13,12},{... | collective-permute-start | bytes 61448 | tf_op jit(solution)/shard_map/ppermute | solution.py:28
  18.1 1.3 %fusion.23 = (f32[2,10,64,1]{3,1,2,0:T(8,128)S(1)}, f32[2,10,64,1]{3,1,2,0:T(8,128)}) fusion(f32[1,10,64,256]{3,1,2,0:T(8,128)S(1)} %get-tuple-element.22, f32[1,10,64,256]{3,1,2,0:T(8,128)S(1)} %get-tuple-element.24), kind=kLoop, calls=%fused_computation.43 | loop fusion | flops 2560 | bytes 1320960 | tf_op jit(solution)/shard_map/stack | solution.py:62
  19.4 0.0 copy-done.1
  19.4 1.5 %copy.30 = f32[2,10,64,1]{2,0,3,1:T(2,128)S(1)} copy(f32[2,10,64,1]{3,1,2,0:T(8,128)} %get-tuple-element.16) | data formatting | bytes 10240 | tf_op jit(solution)/shard_map/slice | solution.py:26
  20.9 0.2 collective-permute-start.1
  21.2 0.3 copy.28
  21.5 4.0 %collective-permute-start = (f32[2,10,64,1]{2,0,3,1:T(2,128)S(1)}, f32[2,10,64,1]{2,0,3,1:T(2,128)S(1)}, u32[]{:S(2)}, u32[]{:S(2)}) collective-permute-start(f32[2,10,64,1]{2,0,3,1:T(2,128)S(1)} %copy.28), channel_id=1, source_target_pairs={{4,0},{8,4},{12,8},{16,12},{20,16},{24,20},{28,24},{0,28},{5,1},{9... | collective-permute-start | bytes 15368 | tf_op jit(solution)/shard_map/ppermute | solution.py:28
  25.5 0.0 collective-permute-done.2
  25.5 0.0 collective-permute-start.3
  25.5 1.6 %fusion.1 = f32[2,10,63,256]{3,1,2,0:T(8,128)} fusion(f32[1,10,64,256]{3,1,2,0:T(8,128)S(1)} %get-tuple-element.23, f32[1,10,64,256]{3,1,2,0:T(8,128)S(1)} %get-tuple-element.24), kind=kLoop, calls=%fused_computation.17 | loop fusion | flops 322560 | bytes 2600960 | tf_op jit(solution)/shard_map/stack | solution.py:63
  27.1 1.2 %collective-permute-done.3 = f32[2,10,256]{2,1,0:T(8,128)S(1)} collective-permute-done((f32[2,10,256]{2,1,0:T(8,128)S(1)}, f32[2,10,256]{2,1,0:T(8,128)S(1)}, u32[]{:S(2)}, u32[]{:S(2)}) %collective-permute-start.3) | collective-permute-done | bytes 20512 | tf_op jit(solution)/shard_map/ppermute | solution.py:15
  28.3 0.6 collective-permute-start.4
  28.9 1.1 %constant_dynamic-slice_fusion = (f32[1,10,64,256]{3,2,1,0:T(8,128)}, f32[1,10,64,256]{3,2,1,0:T(8,128)}) fusion(f32[4,10,64,256]{3,2,1,0:T(8,128)S(1)} %copy-done.8, s32[]{:T(128)S(6)} %select_n.25, s32[]{:T(128)S(6)} %select_n.22), kind=kLoop, calls=%fused_computation.98 | loop fusion | bytes 2621448 | tf_op jit(solution)/shard_map/dynamic_slice | solution.py:56
  30.0 0.0 collective-permute-done
  30.0 1.5 %copy.29 = f32[2,10,64,1]{3,1,2,0:T(8,128)} copy(f32[2,10,64,1]{2,0,3,1:T(2,128)S(1)} %collective-permute-done) | data formatting | bytes 10240 | tf_op jit(solution)/shard_map/ppermute | solution.py:28
  31.5 0.0 collective-permute-done.1
  31.5 1.4 %copy.31 = f32[2,10,64,1]{3,1,2,0:T(8,128)} copy(f32[2,10,64,1]{2,0,3,1:T(2,128)S(1)} %collective-permute-done.1) | data formatting | bytes 10240 | tf_op jit(solution)/shard_map/ppermute | solution.py:25
  32.9 0.3 collective-permute-done.4
  33.2 0.1 rev.6
  33.4 0.0 collective-permute-done.5
  33.4 0.0 collective-permute-done.6
  33.4 0.0 copy-done
  33.4 0.0 copy-done.2
  33.4 0.0 copy-start.5
  33.4 6.1 %fusion.7 = f32[10,64,256]{2,0,1:T(8,128)S(1)} fusion(f32[2,10,63,256]{3,1,2,0:T(8,128)} %fusion.1, f32[2,10,1,256]{3,1,2,0:T(8,128)S(1)} %fusion.47, f32[2,10,1,256]{3,1,2,0:T(8,128)S(1)} %bitcast.115, f32[1,10,64,256]{3,1,2,0:T(8,128)S(1)} %get-tuple-element.23, f32[1,10,64,256]{3,1,2,0:T(8,128)S(1)} %get-tuple-element.24, f32[2,10,64,1]{3,1,2,0:T(8,128)} %copy.31, ...), kind=kOutput, calls=%fused_computation.27 | convolution fusion | flops 25231360 | bytes 10070016 | tf_op jit(solution)/shard_map/ml,mab->lab/dot_general | solution.py:73
  39.6 0.0 copy-start.7
  39.6 0.0 copy-done.5
  39.6 0.0 copy-done.6
  39.6 0.9 %fusion.35 = (f32[1,10,64,256]{3,1,2,0:T(8,128)S(1)}, f32[1,10,64,256]{3,1,2,0:T(8,128)S(1)}, f32[1,10,64,256]{3,1,2,0:T(8,128)S(1)}) fusion(f32[10,64,256]{2,0,1:T(8,128)S(1)} %fusion.7, f32[1,10,64,256]{3,2,1,0:T(8,128)S(1)} %copy-done.6, f32[1,10,64,256]{3,2,1,0:T(8,128)S(1)} %copy-done.5, f32[64,256]{1,0:T(8,128)S(1)} %copy-done.10), kind=kLoop, calls=%fused_computation.75 | loop fusion | flops 491520 | bytes 3997696 | tf_op jit(solution)/shard_map/stack | solution.py:62
  40.5 0.1 copy-done.7
  40.6 0.1 collective-permute-start.9
  40.6 2.4 %collective-permute-start.12 = (f32[2,10,1,256]{3,1,2,0:T(8,128)S(1)}, f32[2,10,1,256]{3,1,2,0:T(8,128)S(1)}, u32[]{:S(2)}, u32[]{:S(2)}) collective-permute-start(f32[2,10,1,256]{3,1,2,0:T(8,128)S(1)} %get-tuple-element.13), channel_id=1, source_target_pairs={{1,0},{2,1},{3,2},{5,4},{6,5},{7,6},{9,8},{10,9},{11,10},{13,12},{... | collective-permute-start | bytes 61448 | tf_op jit(solution)/shard_map/ppermute | solution.py:28
  43.0 0.4 collective-permute-done.9
  43.4 0.9 %collective-permute-start.10 = (f32[2,10,256]{2,1,0:T(8,128)S(1)}, f32[2,10,256]{2,1,0:T(8,128)S(1)}, u32[]{:S(2)}, u32[]{:S(2)}) collective-permute-start(f32[2,10,256]{2,1,0:T(8,128)S(1)} %collective-permute-done.9), channel_id=1, source_target_pairs={{0,8},{4,12},{8,0},{12,4},{16,24},{20,28},{24,16},{28,20},{1,9},{5... | collective-permute-start | bytes 61448 | tf_op jit(solution)/shard_map/ppermute | solution.py:15
  44.3 1.3 %fusion.16 = (f32[2,10,64,1]{3,1,2,0:T(8,128)}, f32[2,10,64,1]{3,1,2,0:T(8,128)S(1)}) fusion(f32[1,10,64,256]{3,1,2,0:T(8,128)S(1)} %get-tuple-element.19, f32[1,10,64,256]{3,1,2,0:T(8,128)S(1)} %get-tuple-element.21), kind=kLoop, calls=%fused_computation.36 | loop fusion | flops 2560 | bytes 1320960 | tf_op jit(solution)/shard_map/stack | solution.py:62
  45.6 0.0 copy-done.3
  45.6 1.5 %copy.40 = f32[2,10,64,1]{2,0,3,1:T(2,128)S(1)} copy(f32[2,10,64,1]{3,1,2,0:T(8,128)} %get-tuple-element.11) | data formatting | bytes 10240 | tf_op jit(solution)/shard_map/slice | solution.py:28
  47.2 0.3 copy.42
  47.5 1.4 %collective-permute-start.8 = (f32[2,10,64,1]{2,0,3,1:T(2,128)S(1)}, f32[2,10,64,1]{2,0,3,1:T(2,128)S(1)}, u32[]{:S(2)}, u32[]{:S(2)}) collective-permute-start(f32[2,10,64,1]{2,0,3,1:T(2,128)S(1)} %copy.42), channel_id=1, source_target_pairs={{0,4},{4,8},{8,12},{12,16},{16,20},{20,24},{24,28},{28,0},{1,5},{5... | collective-permute-start | bytes 15368 | tf_op jit(solution)/shard_map/ppermute | solution.py:25
  49.0 2.7 %collective-permute-start.7 = (f32[2,10,64,1]{2,0,3,1:T(2,128)S(1)}, f32[2,10,64,1]{2,0,3,1:T(2,128)S(1)}, u32[]{:S(2)}, u32[]{:S(2)}) collective-permute-start(f32[2,10,64,1]{2,0,3,1:T(2,128)S(1)} %copy.40), channel_id=1, source_target_pairs={{4,0},{8,4},{12,8},{16,12},{20,16},{24,20},{28,24},{0,28},{5,1},{9... | collective-permute-start | bytes 15368 | tf_op jit(solution)/shard_map/ppermute | solution.py:28
  51.7 0.0 collective-permute-done.10
  51.7 0.0 collective-permute-start.11
  51.7 1.6 %fusion = f32[2,10,63,256]{3,1,2,0:T(8,128)} fusion(f32[1,10,64,256]{3,1,2,0:T(8,128)S(1)} %get-tuple-element.20, f32[1,10,64,256]{3,1,2,0:T(8,128)S(1)} %get-tuple-element.21), kind=kLoop, calls=%fused_computation.16 | loop fusion | flops 322560 | bytes 2600960 | tf_op jit(solution)/shard_map/stack | solution.py:63
  53.3 8.0 %collective-permute-start.13 = (f32[2,10,1,256]{3,1,0,2:T(8,128)S(1)}, f32[2,10,1,256]{3,1,0,2:T(8,128)S(1)}, u32[]{:S(2)}, u32[]{:S(2)}) collective-permute-start(f32[2,10,1,256]{3,1,0,2:T(8,128)S(1)} %bitcast.114), channel_id=1, source_target_pairs={{0,1},{1,2},{2,3},{4,5},{5,6},{6,7},{8,9},{9,10},{10,11},{12,13},{... | collective-permute-start | bytes 61448 | tf_op jit(solution)/shard_map/ppermute | solution.py:25
  61.3 0.0 collective-permute-done.7
  61.3 1.4 %copy.41 = f32[2,10,64,1]{3,1,2,0:T(8,128)} copy(f32[2,10,64,1]{2,0,3,1:T(2,128)S(1)} %collective-permute-done.7) | data formatting | bytes 10240 | tf_op jit(solution)/shard_map/ppermute | solution.py:28
  62.8 0.0 collective-permute-done.8
  62.8 1.4 %copy.43 = f32[2,10,64,1]{3,1,2,0:T(8,128)} copy(f32[2,10,64,1]{2,0,3,1:T(2,128)S(1)} %collective-permute-done.8) | data formatting | bytes 10240 | tf_op jit(solution)/shard_map/ppermute | solution.py:25
  64.2 0.0 collective-permute-done.11
  64.2 0.1 rev.7
  64.3 0.0 collective-permute-done.12
  64.4 0.0 collective-permute-done.13
  64.4 5.5 %fusion.4 = f32[10,64,256]{2,0,1:T(8,128)S(1)} fusion(f32[10,64,256]{2,0,1:T(8,128)} %copy-done.7, f32[2,10,63,256]{3,1,2,0:T(8,128)} %fusion, f32[2,10,1,256]{3,1,2,0:T(8,128)S(1)} %fusion.46, f32[2,10,1,256]{3,1,2,0:T(8,128)S(1)} %bitcast.116, f32[1,10,64,256]{3,1,2,0:T(8,128)S(1)} %get-tuple-element.20, f32[1,10,64,256]{3,1,2,0:T(8,128)S(1)} %get-tuple-element.21, ...), kind=kOutput, calls=%fused_computation.23 | convolution fusion | flops 24903680 | bytes 9643408 | tf_op jit(solution)/shard_map/ml,mab->lab/dot_general | solution.py:73
  69.9 1.2 %copy.50 = f32[10,64,256]{2,1,0:T(8,128)} copy(f32[10,64,256]{2,0,1:T(8,128)S(1)} %fusion.4) | data formatting | bytes 1310720 | tf_op jit(solution)/shard_map/mul | solution.py:74
  (14 shorter events, 0.0 us)
Async XLA Ops:
  0.0 33.4 %copy-start = (f32[10,10]{1,0:T(8,128)S(1)}, f32[10,10]{1,0:T(8,128)}, u32[]{:S(2)}) copy-start(f32[10,10]{1,0:T(8,128)} %param.13) | copy-start | bytes 1204
  6.0 3.1 %copy-start.9 = (f32[10,64,256]{2,1,0:T(8,128)S(1)}, f32[10,64,256]{2,1,0:T(8,128)}, u32[]{:S(2)}) copy-start(f32[10,64,256]{2,1,0:T(8,128)} %param.8) | copy-start | bytes 1966084
  6.0 3.1 %copy-start.10 = (f32[64,256]{1,0:T(8,128)S(1)}, f32[64,256]{1,0:T(8,128)}, u32[]{:S(2)}) copy-start(f32[64,256]{1,0:T(8,128)} %param.12) | copy-start | bytes 196612
  10.3 9.1 %copy-start.1 = (f32[1,10,64,256]{3,1,2,0:T(8,128)}, f32[1,10,64,256]{3,1,2,0:T(8,128)S(1)}, u32[]{:S(2)}) copy-start(f32[1,10,64,256]{3,1,2,0:T(8,128)S(1)} %get-tuple-element.22) | copy-start | bytes 1966084
  10.3 23.1 %collective-permute-start.6 = (f32[2,10,1,256]{3,1,0,2:T(8,128)S(1)}, f32[2,10,1,256]{3,1,0,2:T(8,128)S(1)}, u32[]{:S(2)}, u32[]{:S(2)}) collective-permute-start(f32[2,10,1,256]{3,1,0,2:T(8,128)S(1)} %bitcast.111), channel_id=1, source_target_pairs={{0,1},{1,2},{2,3},{4,5},{5,6},{6,7},{8,9},{9,10},{10,11},{12,13},{... | collective-permute-start | bytes 61448 | tf_op jit(solution)/shard_map/ppermute | solution.py:25
  14.8 10.7 %collective-permute-start.2 = (f32[2,10,256]{2,1,0:T(8,128)S(1)}, f32[2,10,256]{2,1,0:T(8,128)S(1)}, u32[]{:S(2)}, u32[]{:S(2)}) collective-permute-start(f32[2,10,256]{2,1,0:T(8,128)S(1)} %bitcast.112), channel_id=1, source_target_pairs={{0,4},{4,0},{8,12},{12,8},{16,20},{20,16},{24,28},{28,24},{1,5},{5... | collective-permute-start | bytes 61448 | tf_op jit(solution)/shard_map/ppermute | solution.py:15
  16.1 17.2 %collective-permute-start.5 = (f32[2,10,1,256]{3,1,0,2:T(8,128)S(1)}, f32[2,10,1,256]{3,1,0,2:T(8,128)S(1)}, u32[]{:S(2)}, u32[]{:S(2)}) collective-permute-start(f32[2,10,1,256]{3,1,0,2:T(8,128)S(1)} %get-tuple-element.17), channel_id=1, source_target_pairs={{1,0},{2,1},{3,2},{5,4},{6,5},{7,6},{9,8},{10,9},{11,10},{13,12},{... | collective-permute-start | bytes 61448 | tf_op jit(solution)/shard_map/ppermute | solution.py:28
  20.9 10.6 %collective-permute-start.1 = (f32[2,10,64,1]{2,0,3,1:T(2,128)S(1)}, f32[2,10,64,1]{2,0,3,1:T(2,128)S(1)}, u32[]{:S(2)}, u32[]{:S(2)}) collective-permute-start(f32[2,10,64,1]{2,0,3,1:T(2,128)S(1)} %copy.30), channel_id=1, source_target_pairs={{0,4},{4,8},{8,12},{12,16},{16,20},{20,24},{24,28},{28,0},{1,5},{5... | collective-permute-start | bytes 15368 | tf_op jit(solution)/shard_map/ppermute | solution.py:25
  21.5 7.4 %copy-start.8 = (f32[4,10,64,256]{3,2,1,0:T(8,128)S(1)}, f32[4,10,64,256]{3,2,1,0:T(8,128)}, u32[]{:S(2)}) copy-start(f32[4,10,64,256]{3,2,1,0:T(8,128)} %param.9) | copy-start | bytes 7864324
  21.5 8.5 %collective-permute-start = (f32[2,10,64,1]{2,0,3,1:T(2,128)S(1)}, f32[2,10,64,1]{2,0,3,1:T(2,128)S(1)}, u32[]{:S(2)}, u32[]{:S(2)}) collective-permute-start(f32[2,10,64,1]{2,0,3,1:T(2,128)S(1)} %copy.28), channel_id=1, source_target_pairs={{4,0},{8,4},{12,8},{16,12},{20,16},{24,20},{28,24},{0,28},{5,1},{9... | collective-permute-start | bytes 15368 | tf_op jit(solution)/shard_map/ppermute | solution.py:28
  25.5 2.8 %collective-permute-start.3 = (f32[2,10,256]{2,1,0:T(8,128)S(1)}, f32[2,10,256]{2,1,0:T(8,128)S(1)}, u32[]{:S(2)}, u32[]{:S(2)}) collective-permute-start(f32[2,10,256]{2,1,0:T(8,128)S(1)} %collective-permute-done.2), channel_id=1, source_target_pairs={{0,8},{4,12},{8,0},{12,4},{16,24},{20,28},{24,16},{28,20},{1,9},{5... | collective-permute-start | bytes 61448 | tf_op jit(solution)/shard_map/ppermute | solution.py:15
  27.1 6.3 %copy-start.2 = (f32[1,10,64,256]{3,1,2,0:T(8,128)S(1)}, f32[1,10,64,256]{3,1,2,0:T(8,128)}, u32[]{:S(2)}) copy-start(f32[1,10,64,256]{3,1,2,0:T(8,128)} %copy-done.1) | copy-start | bytes 1966084
  28.3 5.0 %collective-permute-start.4 = (f32[2,10,256]{2,1,0:T(8,128)S(1)}, f32[2,10,256]{2,1,0:T(8,128)S(1)}, u32[]{:S(2)}, u32[]{:S(2)}) collective-permute-start(f32[2,10,256]{2,1,0:T(8,128)S(1)} %collective-permute-done.3), channel_id=1, source_target_pairs={{0,16},{4,20},{8,24},{12,28},{16,0},{20,4},{24,8},{28,12},{1,17},{... | collective-permute-start | bytes 61448 | tf_op jit(solution)/shard_map/ppermute | solution.py:15
  33.4 6.1 %copy-start.5 = (f32[1,10,64,256]{3,2,1,0:T(8,128)S(1)}, f32[1,10,64,256]{3,2,1,0:T(8,128)}, u32[]{:S(2)}) copy-start(f32[1,10,64,256]{3,2,1,0:T(8,128)} %get-tuple-element.9) | copy-start | bytes 1966084
  33.4 6.1 %copy-start.6 = (f32[1,10,64,256]{3,2,1,0:T(8,128)S(1)}, f32[1,10,64,256]{3,2,1,0:T(8,128)}, u32[]{:S(2)}) copy-start(f32[1,10,64,256]{3,2,1,0:T(8,128)} %get-tuple-element.28) | copy-start | bytes 1966084
  39.6 1.0 %copy-start.7 = (f32[10,64,256]{2,0,1:T(8,128)}, f32[10,64,256]{2,0,1:T(8,128)S(1)}, u32[]{:S(2)}) copy-start(f32[10,64,256]{2,0,1:T(8,128)S(1)} %fusion.7) | copy-start | bytes 1966084
  40.5 5.1 %copy-start.3 = (f32[1,10,64,256]{3,1,2,0:T(8,128)}, f32[1,10,64,256]{3,1,2,0:T(8,128)S(1)}, u32[]{:S(2)}) copy-start(f32[1,10,64,256]{3,1,2,0:T(8,128)S(1)} %get-tuple-element.19) | copy-start | bytes 1966084
  40.6 2.8 %collective-permute-start.9 = (f32[2,10,256]{2,1,0:T(8,128)S(1)}, f32[2,10,256]{2,1,0:T(8,128)S(1)}, u32[]{:S(2)}, u32[]{:S(2)}) collective-permute-start(f32[2,10,256]{2,1,0:T(8,128)S(1)} %bitcast.113), channel_id=1, source_target_pairs={{0,4},{4,0},{8,12},{12,8},{16,20},{20,16},{24,28},{28,24},{1,5},{5... | collective-permute-start | bytes 61448 | tf_op jit(solution)/shard_map/ppermute | solution.py:15
  40.6 23.7 %collective-permute-start.12 = (f32[2,10,1,256]{3,1,2,0:T(8,128)S(1)}, f32[2,10,1,256]{3,1,2,0:T(8,128)S(1)}, u32[]{:S(2)}, u32[]{:S(2)}) collective-permute-start(f32[2,10,1,256]{3,1,2,0:T(8,128)S(1)} %get-tuple-element.13), channel_id=1, source_target_pairs={{1,0},{2,1},{3,2},{5,4},{6,5},{7,6},{9,8},{10,9},{11,10},{13,12},{... | collective-permute-start | bytes 61448 | tf_op jit(solution)/shard_map/ppermute | solution.py:28
  43.4 8.3 %collective-permute-start.10 = (f32[2,10,256]{2,1,0:T(8,128)S(1)}, f32[2,10,256]{2,1,0:T(8,128)S(1)}, u32[]{:S(2)}, u32[]{:S(2)}) collective-permute-start(f32[2,10,256]{2,1,0:T(8,128)S(1)} %collective-permute-done.9), channel_id=1, source_target_pairs={{0,8},{4,12},{8,0},{12,4},{16,24},{20,28},{24,16},{28,20},{1,9},{5... | collective-permute-start | bytes 61448 | tf_op jit(solution)/shard_map/ppermute | solution.py:15
  47.5 15.2 %collective-permute-start.8 = (f32[2,10,64,1]{2,0,3,1:T(2,128)S(1)}, f32[2,10,64,1]{2,0,3,1:T(2,128)S(1)}, u32[]{:S(2)}, u32[]{:S(2)}) collective-permute-start(f32[2,10,64,1]{2,0,3,1:T(2,128)S(1)} %copy.42), channel_id=1, source_target_pairs={{0,4},{4,8},{8,12},{12,16},{16,20},{20,24},{24,28},{28,0},{1,5},{5... | collective-permute-start | bytes 15368 | tf_op jit(solution)/shard_map/ppermute | solution.py:25
  49.0 12.3 %collective-permute-start.7 = (f32[2,10,64,1]{2,0,3,1:T(2,128)S(1)}, f32[2,10,64,1]{2,0,3,1:T(2,128)S(1)}, u32[]{:S(2)}, u32[]{:S(2)}) collective-permute-start(f32[2,10,64,1]{2,0,3,1:T(2,128)S(1)} %copy.40), channel_id=1, source_target_pairs={{4,0},{8,4},{12,8},{16,12},{20,16},{24,20},{28,24},{0,28},{5,1},{9... | collective-permute-start | bytes 15368 | tf_op jit(solution)/shard_map/ppermute | solution.py:28
  51.7 12.5 %collective-permute-start.11 = (f32[2,10,256]{2,1,0:T(8,128)S(1)}, f32[2,10,256]{2,1,0:T(8,128)S(1)}, u32[]{:S(2)}, u32[]{:S(2)}) collective-permute-start(f32[2,10,256]{2,1,0:T(8,128)S(1)} %collective-permute-done.10), channel_id=1, source_target_pairs={{0,16},{4,20},{8,24},{12,28},{16,0},{20,4},{24,8},{28,12},{1,17},{... | collective-permute-start | bytes 61448 | tf_op jit(solution)/shard_map/ppermute | solution.py:15
  53.3 11.1 %copy-start.4 = (f32[1,10,64,256]{3,1,2,0:T(8,128)S(1)}, f32[1,10,64,256]{3,1,2,0:T(8,128)}, u32[]{:S(2)}) copy-start(f32[1,10,64,256]{3,1,2,0:T(8,128)} %copy-done.3) | copy-start | bytes 1966084
  53.3 11.1 %collective-permute-start.13 = (f32[2,10,1,256]{3,1,0,2:T(8,128)S(1)}, f32[2,10,1,256]{3,1,0,2:T(8,128)S(1)}, u32[]{:S(2)}, u32[]{:S(2)}) collective-permute-start(f32[2,10,1,256]{3,1,0,2:T(8,128)S(1)} %bitcast.114), channel_id=1, source_target_pairs={{0,1},{1,2},{2,3},{4,5},{5,6},{6,7},{8,9},{9,10},{10,11},{12,13},{... | collective-permute-start | bytes 61448 | tf_op jit(solution)/shard_map/ppermute | solution.py:25
where the time goes:
time: 71.5 us; the launch traced here: 71.1 us
  starting transfers between devices  28.1 us (39%)
  local copies, waits for them, and re-layouts  16.9 us (24%)
  matrix products  11.6 us (16%)
  other arithmetic  8.54 us (12%)
  between operations  4.09 us (6%)
  waiting for transfers between devices  1.91 us (3%)
    ppermute x4, starting transfers between devices, with_halo(): lax.ppermute(lax.slice_in_dim(block, block.shape[dim] - width, None, axis...  14.2 us
    dot_general x2, matrix products, shards(): jnp.einsum('ml,mab->lab', level_mixing, adjoint, precision=lax.Precision....  11.6 us
    ppermute x4, starting transfers between devices, with_halo(): lax.ppermute(lax.slice_in_dim(block, 0, width, axis=dim), axis, backward)  11 us
    another operation x4, other arithmetic, shards(): jnp.stack([spread, zonal_flux])  4.72 us
    another operation x3, other arithmetic, shards(): along_lat_src = jnp.stack([spread, merid_flux])  3.14 us
    dynamic_slice x1, local copies, waits for them, and re-layouts, shards(): merid = stored_meridional[chosen]  3.1 us
    ppermute x2, local copies, waits for them, and re-layouts, with_halo(): lax.ppermute(lax.slice_in_dim(block, 0, width, axis=dim), axis, backward)  2.92 us
    ppermute x6, starting transfers between devices, partner(): lax.ppermute(array, axis, [(i, i ^ 1 << distance) for i in range(lax.axis...  2.91 us
  transfers between devices with their start and end apart: 14, of which 3 were waited for; matrix products, arithmetic and copies ran while one was open for 24% of the time, Pallas kernels for 0%

commit v1 on v0

v1 whole, which is shorter than its diff:
```python
import functools

import jax
import jax.numpy as jnp
from jax import lax
from jax.experimental import pallas as pl
from jax.experimental.pallas import tpu as pltpu
from jax.sharding import PartitionSpec as P

TLON = 128
STEPS = 2
LANES = 128
ROWS = 8

advect_scale = 0.25
damping = 0.3

MESH = pl.DeviceIdType.MESH


def kernel(
    lons, lats,
    af_h, q_h, u_h, v_h, d_h, mix, wet, sidx,
    out,
    af, q, u, v, dv, mid, wbuf, col_out, col_in, row_out, row_in,
    load_sem, send_sem, recv_sem,
):
    levels, height, width = af.shape
    store = u.shape[0]
    strips = height // ROWS
    pitch = LANES // strips
    lon = lax.axis_index("lon")
    lat = lax.axis_index("lat")
    east = lax.rem(lon + 1, lons)
    west = lax.rem(lon + lons - 1, lons)
    mirror = lons - 1 - lon
    top = lats - 1

    barrier = pltpu.get_barrier_semaphore()

    def greet(device_id):
        pl.semaphore_signal(barrier, inc=1, device_id=device_id, device_id_type=MESH)

    greet({"lon": east})
    greet({"lon": west})

    @pl.when(lat < top)
    def _():
        greet({"lat": lat + 1})

    folds = (lat == top) & (mirror != east) & (mirror != west)
    four = ((lat > 0) & (lat < top)) | folds

    @pl.when(folds)
    def _():
        greet({"lon": mirror})

    @pl.when(lat > 0)
    def _():
        greet({"lat": lat - 1})

    loads = [(d_h, dv), (af_h, af)]
    loads += [(u_h.at[s], u.at[s]) for s in range(store)]
    loads += [(v_h.at[s], v.at[s]) for s in range(store)]
    loads += [(q_h.at[s], q.at[s]) for s in range(store)]
    loads = [pltpu.make_async_copy(src, dst, load_sem.at[i]) for i, (src, dst) in enumerate(loads)]
    for load in loads:
        load.start()

    for t in range(width // TLON):
        flag = wet[0, t].astype(jnp.float32)
        wbuf[:, t * TLON:(t + 1) * TLON] = jnp.full((ROWS, TLON), flag, jnp.float32)

    @pl.when(lat == 0)
    def _():
        for k in range(STEPS):
            row_in[k, 1] = jnp.zeros(row_in.shape[2:], jnp.float32)

    lane = lax.broadcasted_iota(jnp.int32, (ROWS, LANES), 1)

    def remote(src, dst, send, recv, device_id):
        return pltpu.make_async_remote_copy(
            src_ref=src, dst_ref=dst, send_sem=send, recv_sem=recv,
            device_id=device_id, device_id_type=MESH,
        )

    def copies(k):
        return (
            remote(col_out.at[k, 0], col_in.at[k, 0], send_sem.at[k, 0], recv_sem.at[k, 0], {"lon": west}),
            remote(col_out.at[k, 1], col_in.at[k, 1], send_sem.at[k, 1], recv_sem.at[k, 1], {"lon": east}),
            remote(row_out.at[k, 0], row_in.at[k, 0], send_sem.at[k, 2], recv_sem.at[k, 2], {"lat": lat - 1}),
            remote(row_out.at[k, 1], row_in.at[k, 1], send_sem.at[k, 3], recv_sem.at[k, 3], {"lat": lat + 1}),
            remote(row_out.at[k, 2], row_in.at[k, 0], send_sem.at[k, 4], recv_sem.at[k, 2], {"lon": mirror}),
        )

    def send_edges(k, src, state, first):
        to_west, to_east, to_south, to_north, to_mirror = copies(k)
        for l in range(levels):
            x = src[l, 0:1, :]
            y = src[l, height - 1:height, :]
            if first:
                x = x * wbuf[0:1, :]
                y = y * wbuf[0:1, :]
            vx = advect_scale * v[state, l, 0:1, :]
            vy = advect_scale * v[state, l, height - 1:height, :]
            dy = dv[height - 1:height, :]
            row_out[k, 0, l:l + 1, :] = (dv[0:1, :] + vx) * x
            row_out[k, 1, l:l + 1, :] = (dy - vy) * y
            row_out[k, 2, l:l + 1, :] = (dy + vy) * y

        @pl.when(lat > 0)
        def _():
            to_south.start()

        @pl.when(lat < top)
        def _():
            to_north.start()

        @pl.when(lat == top)
        def _():
            rows = row_out[k, 2]
            padded = rows.shape[0]
            parts = []
            for r in range(padded // ROWS):
                parts.append([
                    jnp.take_along_axis(
                        rows[r * ROWS:(r + 1) * ROWS, t * LANES:(t + 1) * LANES],
                        LANES - 1 - lane, axis=1)
                    for t in range(width // LANES)
                ])
            for r, tiles in enumerate(parts):
                for t, tile in enumerate(tiles):
                    place = width // LANES - 1 - t
                    row_out[k, 2, r * ROWS:(r + 1) * ROWS, place * LANES:(place + 1) * LANES] = tile
            to_mirror.start()

        def pack(j, packed):
            low, high = packed
            rows = pl.ds(pl.multiple_of(j * ROWS, ROWS), ROWS)
            for l in range(levels):
                here = lane == j * pitch + l
                x = src[l, rows, 0:LANES]
                y = src[l, rows, width - LANES:width]
                if first:
                    x = x * wbuf[:, 0:LANES]
                    y = y * wbuf[:, width - LANES:width]
                x = (dv[rows, 0:LANES] + advect_scale * u[state, l, rows, 0:LANES]) * x
                y = (dv[rows, width - LANES:width] - advect_scale * u[state, l, rows, width - LANES:width]) * y
                low = jnp.where(here, jnp.broadcast_to(x[:, 0:1], (ROWS, LANES)), low)
                high = jnp.where(here, jnp.broadcast_to(y[:, LANES - 1:LANES], (ROWS, LANES)), high)
            return low, high

        zero = jnp.zeros((ROWS, LANES), jnp.float32)
        low, high = lax.fori_loop(0, strips, pack, (zero, zero))
        col_out[k, 0] = low
        col_out[k, 1] = high
        to_west.start()
        to_east.start()

    def vertical(src, dst, first):
        def strip(j, _):
            rows = pl.ds(pl.multiple_of(j * ROWS, ROWS), ROWS)
            for t in range(width // LANES):
                cols = slice(t * LANES, (t + 1) * LANES)
                xs = [src[m, rows, cols] for m in range(levels)]
                if first:
                    xs = [x * wbuf[:, cols] for x in xs]
                for l in range(levels):
                    total = xs[0] * mix[0, l]
                    for m in range(1, levels):
                        total = total + xs[m] * mix[m, l]
                    dst[l, rows, cols] = total
            return 0

        lax.fori_loop(0, strips, strip, 0)

    def horizontal(src, dst, state, first):
        row = lax.broadcasted_iota(jnp.int32, (height, width), 0)
        column = lax.broadcasted_iota(jnp.int32, (height, width), 1)

        def level(l, _):
            w = jnp.broadcast_to(wbuf[0:1, :], (height, width))
            x = src[l]
            if first:
                x = x * w
            d = dv[...]
            zonal = advect_scale * u[state, l]
            merid = advect_scale * v[state, l]
            tracer = q[state, l]
            total = dst[l] + x * (1.0 - 4.0 * d - damping * tracer * tracer)
            total += jnp.where(column == width - 1, 0.0, pltpu.roll((d + zonal) * x, width - 1, 1))
            total += jnp.where(column == 0, 0.0, pltpu.roll((d - zonal) * x, 1, 1))
            total += jnp.where(row == height - 1, 0.0, pltpu.roll((d + merid) * x, height - 1, 0))
            total += jnp.where(row == 0, 0.0, pltpu.roll((d - merid) * x, 1, 0))
            dst[l] = w * total
            return 0

        lax.fori_loop(0, levels, level, 0)

    def add_edges(k, dst):
        from_east, from_west, from_north, from_south, _ = copies(k)
        from_north.wait_recv()

        @pl.when(lat > 0)
        def _():
            from_south.wait_recv()

        w = wbuf[0:1, :]
        for l in range(levels):
            dst[l, height - 1:height, :] = dst[l, height - 1:height, :] + w * row_in[k, 0, l:l + 1, :]
            dst[l, 0:1, :] = dst[l, 0:1, :] + w * row_in[k, 1, l:l + 1, :]
        from_east.wait_recv()
        from_west.wait_recv()
        high = col_in[k, 0] * wbuf[:, width - LANES:width]
        low = col_in[k, 1] * wbuf[:, 0:LANES]

        def unpack(j, _):
            rows = pl.ds(pl.multiple_of(j * ROWS, ROWS), ROWS)
            shift = lax.rem(LANES - j * pitch, LANES)
            h = pltpu.roll(high, shift, 1)
            g = pltpu.roll(low, shift, 1)
            for l in range(levels):
                hl = jnp.broadcast_to(h[:, l:l + 1], (ROWS, LANES))
                gl = jnp.broadcast_to(g[:, l:l + 1], (ROWS, LANES))
                cols = slice(width - LANES, width)
                dst[l, rows, cols] = dst[l, rows, cols] + jnp.where(lane == LANES - 1, hl, 0.0)
                cols = slice(0, LANES)
                dst[l, rows, cols] = dst[l, rows, cols] + jnp.where(lane == 0, gl, 0.0)
            return 0

        lax.fori_loop(0, strips, unpack, 0)

    def finish_sends(k):
        to_west, to_east, to_south, to_north, to_mirror = copies(k)
        to_west.wait_send()
        to_east.wait_send()

        @pl.when(lat > 0)
        def _():
            to_south.wait_send()

        @pl.when(lat < top)
        def _():
            to_north.wait_send()

        @pl.when(lat == top)
        def _():
            to_mirror.wait_send()

    for load in loads[:2 + 2 * store]:
        load.wait()

    @pl.when(four)
    def _():
        pl.semaphore_wait(barrier, 4)

    @pl.when(jnp.logical_not(four))
    def _():
        pl.semaphore_wait(barrier, 3)

    state = sidx[STEPS - 1]
    send_edges(0, af, state, True)
    vertical(af, mid, True)
    for load in loads[2 + 2 * store:]:
        load.wait()
    horizontal(af, mid, state, True)
    add_edges(0, mid)

    state = sidx[STEPS - 2]
    send_edges(1, mid, state, False)
    vertical(mid, out, False)
    horizontal(mid, out, state, False)
    add_edges(1, out)
    finish_sends(0)
    finish_sends(1)


def shards(lons, lats, af, q, u, v, d, mix, wet, sidx):
    levels, height, width = af.shape
    store = u.shape[0]
    padded = -(-levels // ROWS) * ROWS
    f32 = jnp.float32
    hbm = pl.BlockSpec(memory_space=pltpu.HBM)
    smem = pl.BlockSpec(memory_space=pltpu.SMEM)
    vmem = pl.BlockSpec(memory_space=pltpu.VMEM)
    cells = levels * height * width
    return pl.pallas_call(
        functools.partial(kernel, lons, lats),
        out_shape=jax.ShapeDtypeStruct((levels, height, width), f32),
        in_specs=[hbm] * 5 + [smem] * 3,
        out_specs=vmem,
        scratch_shapes=[
            pltpu.VMEM((levels, height, width), f32),
            pltpu.VMEM((store, levels, height, width), f32),
            pltpu.VMEM((store, levels, height, width), f32),
            pltpu.VMEM((store, levels, height, width), f32),
            pltpu.VMEM((height, width), f32),
            pltpu.VMEM((levels, height, width), f32),
            pltpu.VMEM((ROWS, width), f32),
            pltpu.VMEM((STEPS, 2, ROWS, LANES), f32),
            pltpu.VMEM((STEPS, 2, ROWS, LANES), f32),
            pltpu.VMEM((STEPS, 3, padded, width), f32),
            pltpu.VMEM((STEPS, 2, padded, width), f32),
            pltpu.SemaphoreType.DMA((2 + 3 * store,)),
            pltpu.SemaphoreType.DMA((STEPS, 5)),
            pltpu.SemaphoreType.DMA((STEPS, 4)),
        ],
        compiler_params=pltpu.CompilerParams(
            collective_id=0, has_side_effects=True, vmem_limit_bytes=56 * 1024 * 1024
        ),
        cost_estimate=pl.CostEstimate(
            flops=90 * cells, bytes_accessed=4 * cells * (3 * store + 2), transcendentals=0
        ),
    )(af, q, u, v, d, mix, wet, sidx)


def solution(mesh):
    return jax.shard_map(
        functools.partial(shards, mesh.shape["lon"], mesh.shape["lat"]),
        mesh=mesh,
        in_specs=(
            P(None, "lat", "lon"),
            P(None, None, "lat", "lon"),
            P(None, None, "lat", "lon"),
            P(None, None, "lat", "lon"),
            P("lat", "lon"),
            P(),
            P("lat", "lon"),
            P(),
        ),
        out_specs=P(None, "lat", "lon"),
        check_vma=False,
    )
```

time: 71.5 us -> 22.3 us (0.31)
  the two profiles are of different devices: /device:TPU:1 before, /device:TPU:0 now
where the time goes in v1:
time: 22.3 us; the launch traced here: 22.1 us
  Pallas kernels  20.2 us (91%)
  local copies, waits for them, and re-layouts  1.97 us (9%)
    pallas_call x1, Pallas kernels, shards(): pl.pallas_call(functools.partial(kernel, lons, lats), out_shape=jax.Shape...  20.2 us
    unnamed x1, local copies, waits for them, and re-layouts  1.97 us

profile of v1, /device:TPU:0, one launch (start us, length us, event | category | flops | bytes accessed | tf_op | source)
XLA Modules:
  0.0 22.1 jit_solution(7039422089234685639)
XLA Ops:
  0.0 20.2 %shard_map.82 = f32[10,64,256]{2,1,0:T(8,128)} custom-call(f32[10,64,256]{2,1,0:T(8,128)} %af_h.1, f32[4,10,64,256]{3,2,1,0:T(8,128)} %q_h.1, f32[4,10,64,256]{3,2,1,0:T(8,128)} %u_h.1, f32[4,10,64,256]{3,2,1,0:T(8,128)} %v_h.1, f32[64,256]{1,0:T(8,128)} %d_h.1, f32[10,10]{1,0:T(8,128)} %mix.1, s32[1,2]{1,0:T(1,128)} %wet.1, s32[2]{0:T(128)} %sidx.1), custom_call_target="tpu_custom_call" | custom-call | flops 14745600 | bytes 9175040 | tf_op jit(solution)/shard_map/pallas_call | solution.py:287
  20.2 2.0 %copy.10 = f32[10,64,256]{2,1,0:T(8,128)} copy(f32[10,64,256]{2,1,0:T(8,128)} %shard_map.82) | data formatting | bytes 1310720

commit v2 on v1

--- a/solution.py
+++ b/solution.py
@@ -29,6 +29,7 @@
     store = u.shape[0]
     strips = height // ROWS
     pitch = LANES // strips
+    padded = row_in.shape[2] - ROWS
     lon = lax.axis_index("lon")
     lat = lax.axis_index("lat")
     east = lax.rem(lon + 1, lons)
@@ -64,7 +65,8 @@
     loads += [(v_h.at[s], v.at[s]) for s in range(store)]
     loads += [(q_h.at[s], q.at[s]) for s in range(store)]
     loads = [pltpu.make_async_copy(src, dst, load_sem.at[i]) for i, (src, dst) in enumerate(loads)]
-    for load in loads:
+    early = loads[:2 + store]
+    for load in early:
         load.start()
 
     for t in range(width // TLON):
@@ -77,6 +79,7 @@
             row_in[k, 1] = jnp.zeros(row_in.shape[2:], jnp.float32)
 
     lane = lax.broadcasted_iota(jnp.int32, (ROWS, LANES), 1)
+    sublane = lax.broadcasted_iota(jnp.int32, (ROWS, LANES), 0)
 
     def remote(src, dst, send, recv, device_id):
         return pltpu.make_async_remote_copy(
@@ -93,8 +96,56 @@
             remote(row_out.at[k, 2], row_in.at[k, 0], send_sem.at[k, 4], recv_sem.at[k, 2], {"lon": mirror}),
         )
 
-    def send_edges(k, src, state, first):
-        to_west, to_east, to_south, to_north, to_mirror = copies(k)
+    def pack(column):
+        packed = jnp.zeros((ROWS, LANES), jnp.float32)
+        for j in range(strips):
+            for l in range(levels):
+                tile, place = column(l, slice(j * ROWS, (j + 1) * ROWS))
+                spread = jnp.broadcast_to(tile[:, place:place + 1], (ROWS, LANES))
+                packed = jnp.where(lane == j * pitch + l, spread, packed)
+        return packed,
+
+    def west_flux(state, apply):
+        def column(l, rows):
+            rate = dv[rows, 0:LANES] + advect_scale * u[state, l, rows, 0:LANES]
+            if apply:
+                rate = rate * (af[l, rows, 0:LANES] * wbuf[:, 0:LANES])
+            return rate, 0
+        return column
+
+    def east_flux(state, apply):
+        cols = slice(width - LANES, width)
+
+        def column(l, rows):
+            rate = dv[rows, cols] - advect_scale * u[state, l, rows, cols]
+            if apply:
+                rate = rate * (af[l, rows, cols] * wbuf[:, cols])
+            return rate, LANES - 1
+        return column
+
+    def send_columns(k, low, high):
+        to_west, to_east, *_ = copies(k)
+        col_out[k, 0] = low
+        col_out[k, 1] = high
+        to_west.start()
+        to_east.start()
+
+    def corner_rows(k, slot, strip, r, swap):
+        low = jnp.zeros((ROWS, LANES), jnp.float32)
+        high = low
+        for l in range(levels):
+            here = (lane == strip * pitch + l) & (sublane == r)
+            x = jnp.broadcast_to(row_out[k, slot, l:l + 1, 0:LANES][:, 0:1], (ROWS, LANES))
+            y = jnp.broadcast_to(row_out[k, slot, l:l + 1, width - LANES:width][:, LANES - 1:LANES], (ROWS, LANES))
+            low = jnp.where(here, x, low)
+            high = jnp.where(here, y, high)
+        if swap:
+            low, high = high, low
+        row_out[k, slot, padded:padded + ROWS, 0:LANES] = low
+        row_out[k, slot, padded:padded + ROWS, width - LANES:width] = high
+
+    def send_rows(k, src, state, first):
+        _, _, to_south, to_north, to_mirror = copies(k)
         for l in range(levels):
             x = src[l, 0:1, :]
             y = src[l, height - 1:height, :]
@@ -108,6 +159,10 @@
             row_out[k, 1, l:l + 1, :] = (dy - vy) * y
             row_out[k, 2, l:l + 1, :] = (dy + vy) * y
 
+        if first:
+            corner_rows(k, 0, strips - 1, ROWS - 1, False)
+            corner_rows(k, 1, 0, 0, False)
+
         @pl.when(lat > 0)
         def _():
             to_south.start()
@@ -118,8 +173,9 @@
 
         @pl.when(lat == top)
         def _():
-            rows = row_out[k, 2]
-            padded = rows.shape[0]
+            if first:
+                corner_rows(k, 2, strips - 1, ROWS - 1, True)
+            rows = row_out[k, 2, 0:padded, :]
             parts = []
             for r in range(padded // ROWS):
                 parts.append([
@@ -133,29 +189,6 @@
                     place = width // LANES - 1 - t
                     row_out[k, 2, r * ROWS:(r + 1) * ROWS, place * LANES:(place + 1) * LANES] = tile
             to_mirror.start()
-
-        def pack(j, packed):
-            low, high = packed
-            rows = pl.ds(pl.multiple_of(j * ROWS, ROWS), ROWS)
-            for l in range(levels):
-                here = lane == j * pitch + l
-                x = src[l, rows, 0:LANES]
-                y = src[l, rows, width - LANES:width]
-                if first:
-                    x = x * wbuf[:, 0:LANES]
-                    y = y * wbuf[:, width - LANES:width]
-                x = (dv[rows, 0:LANES] + advect_scale * u[state, l, rows, 0:LANES]) * x
-                y = (dv[rows, width - LANES:width] - advect_scale * u[state, l, rows, width - LANES:width]) * y
-                low = jnp.where(here, jnp.broadcast_to(x[:, 0:1], (ROWS, LANES)), low)
-                high = jnp.where(here, jnp.broadcast_to(y[:, LANES - 1:LANES], (ROWS, LANES)), high)
-            return low, high
-
-        zero = jnp.zeros((ROWS, LANES), jnp.float32)
-        low, high = lax.fori_loop(0, strips, pack, (zero, zero))
-        col_out[k, 0] = low
-        col_out[k, 1] = high
-        to_west.start()
-        to_east.start()
 
     def vertical(src, dst, first):
         def strip(j, _):
@@ -172,7 +205,7 @@
                     dst[l, rows, cols] = total
             return 0
 
-        lax.fori_loop(0, strips, strip, 0)
+        lax.fori_loop(0, strips, strip, 0, unroll=True)
 
     def horizontal(src, dst, state, first):
         row = lax.broadcasted_iota(jnp.int32, (height, width), 0)
@@ -195,9 +228,9 @@
             dst[l] = w * total
             return 0
 
-        lax.fori_loop(0, levels, level, 0)
-
-    def add_edges(k, dst):
+        lax.fori_loop(0, levels, level, 0, unroll=True)
+
+    def wait_edges(k):
         from_east, from_west, from_north, from_south, _ = copies(k)
         from_north.wait_recv()
 
@@ -205,30 +238,31 @@
         def _():
             from_south.wait_recv()
 
+        from_east.wait_recv()
+        from_west.wait_recv()
+
+    def add_edges(k, dst):
         w = wbuf[0:1, :]
         for l in range(levels):
             dst[l, height - 1:height, :] = dst[l, height - 1:height, :] + w * row_in[k, 0, l:l + 1, :]
             dst[l, 0:1, :] = dst[l, 0:1, :] + w * row_in[k, 1, l:l + 1, :]
-        from_east.wait_recv()
-        from_west.wait_recv()
         high = col_in[k, 0] * wbuf[:, width - LANES:width]
         low = col_in[k, 1] * wbuf[:, 0:LANES]
-
-        def unpack(j, _):
-            rows = pl.ds(pl.multiple_of(j * ROWS, ROWS), ROWS)
-            shift = lax.rem(LANES - j * pitch, LANES)
-            h = pltpu.roll(high, shift, 1)
-            g = pltpu.roll(low, shift, 1)
+        first_cols = slice(0, LANES)
+        last_cols = slice(width - LANES, width)
+        for j in range(strips):
+            rows = slice(j * ROWS, (j + 1) * ROWS)
+            news = []
             for l in range(levels):
-                hl = jnp.broadcast_to(h[:, l:l + 1], (ROWS, LANES))
-                gl = jnp.broadcast_to(g[:, l:l + 1], (ROWS, LANES))
-                cols = slice(width - LANES, width)
-                dst[l, rows, cols] = dst[l, rows, cols] + jnp.where(lane == LANES - 1, hl, 0.0)
-                cols = slice(0, LANES)
-                dst[l, rows, cols] = dst[l, rows, cols] + jnp.where(lane == 0, gl, 0.0)
-            return 0
-
-        lax.fori_loop(0, strips, unpack, 0)
+                at = j * pitch + l
+                g = jnp.broadcast_to(low[:, at:at + 1], (ROWS, LANES))
+                h = jnp.broadcast_to(high[:, at:at + 1], (ROWS, LANES))
+                news.append((
+                    dst[l, rows, first_cols] + jnp.where(lane == 0, g, 0.0),
+                    dst[l, rows, last_cols] + jnp.where(lane == LANES - 1, h, 0.0)))
+            for l, (g, h) in enumerate(news):
+                dst[l, rows, first_cols] = g
+                dst[l, rows, last_cols] = h
 
     def finish_sends(k):
         to_west, to_east, to_south, to_north, to_mirror = copies(k)
@@ -247,8 +281,10 @@
         def _():
             to_mirror.wait_send()
 
-    for load in loads[:2 + 2 * store]:
+    for load in early:
         load.wait()
+    for load in loads[2 + store:]:
+        load.start()
 
     @pl.when(four)
     def _():
@@ -258,18 +294,31 @@
     def _():
         pl.semaphore_wait(barrier, 3)
 
-    state = sidx[STEPS - 1]
-    send_edges(0, af, state, True)
+    first = sidx[STEPS - 1]
+    second = sidx[STEPS - 2]
+    send_columns(0, *pack(west_flux(first, True)), *pack(east_flux(first, True)))
+    for load in loads[2 + store:2 + 2 * store]:
+        load.wait()
+    send_rows(0, af, first, True)
     vertical(af, mid, True)
     for load in loads[2 + 2 * store:]:
         load.wait()
-    horizontal(af, mid, state, True)
+    horizontal(af, mid, first, True)
+
+    low_part, = pack(lambda l, rows: (mid[l, rows, 0:LANES], 0))
+    high_part, = pack(lambda l, rows: (mid[l, rows, width - LANES:width], LANES - 1))
+    low_rate, = pack(west_flux(second, False))
+    high_rate, = pack(east_flux(second, False))
+    wait_edges(0)
+    corners = row_in[0, 0, padded:padded + ROWS, :] + row_in[0, 1, padded:padded + ROWS, :]
+    low_part += wbuf[:, 0:LANES] * (col_in[0, 1] + corners[:, 0:LANES])
+    high_part += wbuf[:, width - LANES:width] * (col_in[0, 0] + corners[:, width - LANES:width])
+    send_columns(1, low_rate * low_part, high_rate * high_part)
     add_edges(0, mid)
-
-    state = sidx[STEPS - 2]
-    send_edges(1, mid, state, False)
+    send_rows(1, mid, second, False)
     vertical(mid, out, False)
-    horizontal(mid, out, state, False)
+    horizontal(mid, out, second, False)
+    wait_edges(1)
     add_edges(1, out)
     finish_sends(0)
     finish_sends(1)
@@ -286,7 +335,7 @@
     cells = levels * height * width
     return pl.pallas_call(
         functools.partial(kernel, lons, lats),
-        out_shape=jax.ShapeDtypeStruct((levels, height, width), f32),
+        out_shape=pltpu.VMEM((levels, height, width), f32),
         in_specs=[hbm] * 5 + [smem] * 3,
         out_specs=vmem,
         scratch_shapes=[
@@ -299,8 +348,8 @@
             pltpu.VMEM((ROWS, width), f32),
             pltpu.VMEM((STEPS, 2, ROWS, LANES), f32),
             pltpu.VMEM((STEPS, 2, ROWS, LANES), f32),
-            pltpu.VMEM((STEPS, 3, padded, width), f32),
-            pltpu.VMEM((STEPS, 2, padded, width), f32),
+            pltpu.VMEM((STEPS, 3, padded + ROWS, width), f32),
+            pltpu.VMEM((STEPS, 2, padded + ROWS, width), f32),
             pltpu.SemaphoreType.DMA((2 + 3 * store,)),
             pltpu.SemaphoreType.DMA((STEPS, 5)),
             pltpu.SemaphoreType.DMA((STEPS, 4)),

time: 22.3 us -> 16.6 us (0.74)
  Pallas kernels: 20.2 us -> 15.6 us
  local copies, waits for them, and re-layouts: 1.97 us -> 0.84 us
    pallas_call x1, Pallas kernels: 20.2 us -> 15.6 us  [shards(): pl.pallas_call(functools.partial(kernel, lons, lats), out_shape=pltpu.VME...]
    unnamed x1, local copies, waits for them, and re-layouts: 1.97 us -> 0.84 us
where the time goes in v2:
time: 16.6 us; the launch traced here: 16.4 us
  Pallas kernels  15.6 us (94%)
  local copies, waits for them, and re-layouts  0.84 us (5%)
    pallas_call x1, Pallas kernels, shards(): pl.pallas_call(functools.partial(kernel, lons, lats), out_shape=pltpu.VME...  15.6 us
    unnamed x1, local copies, waits for them, and re-layouts  0.84 us

profile of v2, /device:TPU:0, one launch (start us, length us, event | category | flops | bytes accessed | tf_op | source)
XLA Modules:
  0.0 16.4 jit_solution(1545280047380352905)
XLA Ops:
  0.0 15.6 %shard_map.82 = f32[10,64,256]{2,1,0:T(8,128)S(1)} custom-call(f32[10,64,256]{2,1,0:T(8,128)} %af_h.1, f32[4,10,64,256]{3,2,1,0:T(8,128)} %q_h.1, f32[4,10,64,256]{3,2,1,0:T(8,128)} %u_h.1, f32[4,10,64,256]{3,2,1,0:T(8,128)} %v_h.1, f32[64,256]{1,0:T(8,128)} %d_h.1, f32[10,10]{1,0:T(8,128)} %mix.1, s32[1,2]{1,0:T(1,128)} %wet.1, s32[2]{0:T(128)} %sidx.1), custom_call_target="tpu_custom_call" | custom-call | flops 14745600 | bytes 9175040 | tf_op jit(solution)/shard_map/pallas_call | solution.py:336
  15.6 0.8 %copy.10 = f32[10,64,256]{2,1,0:T(8,128)} copy(f32[10,64,256]{2,1,0:T(8,128)S(1)} %shard_map.82) | data formatting | bytes 1310720

commit v3 on v2

--- a/solution.py
+++ b/solution.py
@@ -230,22 +230,26 @@
 
         lax.fori_loop(0, levels, level, 0, unroll=True)
 
-    def wait_edges(k):
-        from_east, from_west, from_north, from_south, _ = copies(k)
+    def wait_rows(k):
+        _, _, from_north, from_south, _ = copies(k)
         from_north.wait_recv()
 
         @pl.when(lat > 0)
         def _():
             from_south.wait_recv()
 
+    def wait_columns(k):
+        from_east, from_west, *_ = copies(k)
         from_east.wait_recv()
         from_west.wait_recv()
 
-    def add_edges(k, dst):
+    def add_rows(k, dst):
         w = wbuf[0:1, :]
         for l in range(levels):
             dst[l, height - 1:height, :] = dst[l, height - 1:height, :] + w * row_in[k, 0, l:l + 1, :]
             dst[l, 0:1, :] = dst[l, 0:1, :] + w * row_in[k, 1, l:l + 1, :]
+
+    def add_columns(k, dst):
         high = col_in[k, 0] * wbuf[:, width - LANES:width]
         low = col_in[k, 1] * wbuf[:, 0:LANES]
         first_cols = slice(0, LANES)
@@ -309,18 +313,24 @@
     high_part, = pack(lambda l, rows: (mid[l, rows, width - LANES:width], LANES - 1))
     low_rate, = pack(west_flux(second, False))
     high_rate, = pack(east_flux(second, False))
-    wait_edges(0)
+    wait_rows(0)
     corners = row_in[0, 0, padded:padded + ROWS, :] + row_in[0, 1, padded:padded + ROWS, :]
-    low_part += wbuf[:, 0:LANES] * (col_in[0, 1] + corners[:, 0:LANES])
-    high_part += wbuf[:, width - LANES:width] * (col_in[0, 0] + corners[:, width - LANES:width])
+    low_part += wbuf[:, 0:LANES] * corners[:, 0:LANES]
+    high_part += wbuf[:, width - LANES:width] * corners[:, width - LANES:width]
+    add_rows(0, mid)
+    wait_columns(0)
+    low_part += wbuf[:, 0:LANES] * col_in[0, 1]
+    high_part += wbuf[:, width - LANES:width] * col_in[0, 0]
     send_columns(1, low_rate * low_part, high_rate * high_part)
-    add_edges(0, mid)
+    add_columns(0, mid)
     send_rows(1, mid, second, False)
     vertical(mid, out, False)
     horizontal(mid, out, second, False)
-    wait_edges(1)
-    add_edges(1, out)
+    wait_rows(1)
+    add_rows(1, out)
     finish_sends(0)
+    wait_columns(1)
+    add_columns(1, out)
     finish_sends(1)
 
 

time: 16.6 us -> 16.6 us (level)
  no operation moved by 1% of the time
where the time goes in v3:
time: 16.6 us; the launch traced here: 16.4 us
  Pallas kernels  15.6 us (94%)
  local copies, waits for them, and re-layouts  0.84 us (5%)
    pallas_call x1, Pallas kernels, shards(): pl.pallas_call(functools.partial(kernel, lons, lats), out_shape=pltpu.VME...  15.6 us
    unnamed x1, local copies, waits for them, and re-layouts  0.84 us

profile of v3, /device:TPU:0, one launch (start us, length us, event | category | flops | bytes accessed | tf_op | source)
XLA Modules:
  0.0 16.4 jit_solution(15996569655377229550)
XLA Ops:
  0.0 15.6 %shard_map.82 = f32[10,64,256]{2,1,0:T(8,128)S(1)} custom-call(f32[10,64,256]{2,1,0:T(8,128)} %af_h.1, f32[4,10,64,256]{3,2,1,0:T(8,128)} %q_h.1, f32[4,10,64,256]{3,2,1,0:T(8,128)} %u_h.1, f32[4,10,64,256]{3,2,1,0:T(8,128)} %v_h.1, f32[64,256]{1,0:T(8,128)} %d_h.1, f32[10,10]{1,0:T(8,128)} %mix.1, s32[1,2]{1,0:T(1,128)} %wet.1, s32[2]{0:T(128)} %sidx.1), custom_call_target="tpu_custom_call" | custom-call | flops 14745600 | bytes 9175040 | tf_op jit(solution)/shard_map/pallas_call | solution.py:346
  15.6 0.8 %copy.10 = f32[10,64,256]{2,1,0:T(8,128)} copy(f32[10,64,256]{2,1,0:T(8,128)S(1)} %shard_map.82) | data formatting | bytes 1310720
